TPU v7x, 32 devices: a whole 2x2x4 slice. The times are simulated.
32 devices in a mesh: dp: 4 (over y, core), ctx: 4 (over z), tp: 2 (over x).
Axes of the slice: x: 2, y: 2, z: 4, core: 2. Of those that a mesh axis runs over, the one named last changes fastest.
Arguments:
- tokens: bfloat16 [8, 1536, 2048], P('dp', ('ctx', 'tp')), may hold values from -6 to 6
- cotangent: bfloat16 [8, 1536, 2048], P('dp', ('ctx', 'tp')), may hold values from -6 to 6
- lengths: int32 [8, 3], P('dp'), may hold values from 129 to 1024, as said below
- head_counts: int32 [2], replicated, may hold values from 8 to 12, as said below
- norm1_gain: float32 [2048], replicated, may hold values from 0.25 to 1.75
- norm2_gain: float32 [2048], replicated, may hold values from 0.25 to 1.75
- q_gain: float32 [64], replicated, may hold values from 0.25 to 1.75
- k_gain: float32 [64], replicated, may hold values from 0.25 to 1.75
- w_query: bfloat16 [2048, 1536], P(('dp', 'ctx'), 'tp'), may hold values from -0.125 to 0.125
- w_key: bfloat16 [2048, 320], replicated, may hold values from -0.125 to 0.125
- w_value: bfloat16 [2048, 320], replicated, may hold values from -0.125 to 0.125
- w_out: bfloat16 [1536, 2048], P('tp', ('dp', 'ctx')), may hold values from -1.25 to 1.25
- w_gate: bfloat16 [2048, 8192], P(('dp', 'ctx'), 'tp'), may hold values from -0.125 to 0.125
- w_up: bfloat16 [2048, 8192], P(('dp', 'ctx'), 'tp'), may hold values from -0.125 to 0.125
- w_down: bfloat16 [8192, 2048], P('tp', ('dp', 'ctx')), may hold values from -0.0625 to 0.0625
Outputs:
- output: bfloat16 [8, 1536, 2048], P('dp', ('ctx', 'tp'))
- d_input: float32 [8, 1536, 2048], P('dp', ('ctx', 'tp'))
- d_norm1: float32 [2048], replicated
- d_norm2: float32 [2048], replicated
- d_qgain: float32 [64], replicated
- d_kgain: float32 [64], replicated
- d_query: float32 [2048, 1536], P(('dp', 'ctx'), 'tp')
- d_key: float32 [2048, 320], replicated
- d_value: float32 [2048, 320], replicated
- d_out: float32 [1536, 2048], P('tp', ('dp', 'ctx'))
- d_gate: float32 [2048, 8192], P(('dp', 'ctx'), 'tp')
- d_up: float32 [2048, 8192], P(('dp', 'ctx'), 'tp')
- d_down: float32 [8192, 2048], P('tp', ('dp', 'ctx'))
Inputs may be any that keep to these rules, and one draw needn't show every extreme that they name: `lengths`: each packed row of 1536 tokens holds three documents: the middle one has 1024 tokens, starts before token 384 and ends after token 1152; the first and the last sum to 512. The counts sum to 20; index t of tp holds the query heads offset_t to offset_t + head_counts[t] - 1, offset_t being the sum over lower indices; some index holds 12.
All inputs are finite; a program needn't handle non-finite values.
Results may differ from a plain program's by a relative error of at most 0.019.
Values may be sent and summed in bfloat16 or wider, within the bound.
No kernel may reach another device: no remote copies, remote signals or barrier semaphores. Data moves between devices by JAX's collectives and lax.ppermute only.
A program may use at most 640 MiB of HBM per device.

v0:
```python
import math
import jax
import jax.numpy as jnp
from jax import lax
from jax.sharding import PartitionSpec as P

HEADS = 20
KVH = 5
HEAD_DIM = 64
EPSILON = 1e-05
THETA = 10000.0
MASKED = -1e30


def rms_norm(value_tensor, gain):
    return (
        value_tensor
        * lax.rsqrt(jnp.mean(value_tensor * value_tensor, axis=-1, keepdims=True) + EPSILON)
        * gain
    )


def rotary(value_tensor, positions):
    half_width = value_tensor.shape[-1] // 2
    indices = jnp.arange(half_width).astype(jnp.float32)
    frequency = jnp.exp(indices * (-2.0 * math.log(THETA) / value_tensor.shape[-1]))
    angles = positions.astype(jnp.float32)[:, None] * frequency[None, :]
    cosine = jnp.cos(angles)[:, None, :]
    sine_of = jnp.sin(angles)[:, None, :]
    first_half = value_tensor[..., :half_width]
    second_half = value_tensor[..., half_width:]
    return jnp.concatenate(
        [first_half * cosine - second_half * sine_of, first_half * sine_of + second_half * cosine],
        axis=-1,
    )


def head_path(projected, gain, positions):
    shaped = projected.reshape(projected.shape[0], projected.shape[1] // HEAD_DIM, HEAD_DIM)
    return rotary(rms_norm(shaped, gain), positions)


def plain_dot(left, right):
    return jnp.dot(left, right, preferred_element_type=jnp.float32)


def dot_last(left, right):
    return lax.dot_general(
        left, right, (((1,), (1,)), ((), ())), preferred_element_type=jnp.float32
    )


def dot_first(left, right):
    return lax.dot_general(
        left, right, (((0,), (0,)), ((), ())), preferred_element_type=jnp.float32
    )


def gather_rows(value_tensor):
    gathered = lax.all_gather(value_tensor, "tp", axis=1, tiled=True)
    return gathered.reshape(gathered.shape[0] * gathered.shape[1], gathered.shape[2])


def sum_rows(term_fn, row_count):
    return lax.psum_scatter(
        term_fn(jnp.int32(0), row_count * lax.axis_size("tp")),
        "tp",
        scatter_dimension=0,
        tiled=True,
    )


def tp_block(value_tensor, count, seq_rows):
    row_total = value_tensor.shape[0]
    width = value_tensor.shape[2]
    span = count // row_total
    block = value_tensor
    block = block.reshape(row_total, span // seq_rows, seq_rows, width)
    return jnp.swapaxes(block, 0, 1).reshape(count, width)


def slot_table(head_counts, slot_count):
    tp_index = lax.axis_index("tp")
    ranks = jnp.arange(head_counts.shape[0])
    offset = jnp.sum(jnp.where(ranks < tp_index, head_counts, 0))
    held = jnp.sum(jnp.where(ranks == tp_index, head_counts, 0))
    slot_ids = jnp.arange(slot_count)
    valid = (slot_ids < held).astype(jnp.float32)
    kv_head = jnp.minimum((offset + slot_ids) // (HEADS // KVH), KVH - 1)
    select = (jnp.arange(KVH)[:, None] == kv_head[None, :]).astype(jnp.bfloat16)
    return (valid, select)


def doc_table(lengths, row_length):
    doc_ends = jnp.cumsum(lengths, axis=1)
    doc_starts = doc_ends - lengths
    token_places = jnp.arange(row_length)[None, :]
    doc_ids = (token_places >= doc_ends[:, 0:1]).astype(jnp.int32) + (
        token_places >= doc_ends[:, 1:2]
    ).astype(jnp.int32)
    begins = jnp.where(
        doc_ids == 0,
        doc_starts[:, 0:1],
        jnp.where(doc_ids == 1, doc_starts[:, 1:2], doc_starts[:, 2:3]),
    )
    return (doc_ids, token_places - begins)


def body(
    tokens,
    cotangent,
    lengths,
    head_counts,
    norm1_gain,
    norm2_gain,
    q_gain,
    k_gain,
    w_query,
    w_key,
    w_value,
    w_out,
    w_gate,
    w_up,
    w_down,
):
    row_total = tokens.shape[0]
    seq_rows = tokens.shape[1]
    stretch_rows = seq_rows * lax.axis_size("tp")
    row_length = stretch_rows * lax.axis_size("ctx")
    local_rows = row_total * seq_rows
    flat_rows = row_total * stretch_rows
    slot_count = w_query.shape[1] // HEAD_DIM
    model_width = w_key.shape[0]
    scale = HEAD_DIM ** (-0.5)
    valid, select = slot_table(head_counts, slot_count)
    doc_ids, positions = doc_table(lengths, row_length)
    own_start = lax.axis_index("ctx") * stretch_rows
    own_docs = lax.dynamic_slice_in_dim(doc_ids, own_start, stretch_rows, 1)
    own_positions = lax.dynamic_slice_in_dim(positions, own_start, stretch_rows, 1).reshape(
        flat_rows
    )
    own_places = own_start + jnp.arange(stretch_rows)
    allowed = (own_docs[:, :, None] == doc_ids[:, None, :]) & (
        own_places[None, :, None] >= jnp.arange(row_length)[None, None, :]
    )
    query_full, out_full, gate_full, up_full, down_full = (
        lax.all_gather(w_query, ("dp", "ctx"), axis=0, tiled=True),
        lax.all_gather(w_out, ("dp", "ctx"), axis=1, tiled=True),
        lax.all_gather(w_gate, ("dp", "ctx"), axis=0, tiled=True),
        lax.all_gather(w_up, ("dp", "ctx"), axis=0, tiled=True),
        lax.all_gather(w_down, ("dp", "ctx"), axis=1, tiled=True),
    )
    key_slots = (
        jnp.einsum(
            "dkh,ks->dsh",
            w_key.reshape(model_width, KVH, HEAD_DIM),
            select,
            preferred_element_type=jnp.float32,
        )
        .astype(jnp.bfloat16)
        .reshape(model_width, slot_count * HEAD_DIM)
    )
    value_slots = (
        jnp.einsum(
            "dkh,ks->dsh",
            w_value.reshape(model_width, KVH, HEAD_DIM),
            select,
            preferred_element_type=jnp.float32,
        )
        .astype(jnp.bfloat16)
        .reshape(model_width, slot_count * HEAD_DIM)
    )

    def by_slot(value_tensor, length):
        return jnp.moveaxis(value_tensor.reshape(row_total, length, slot_count, HEAD_DIM), 2, 1)

    def by_rows(value_tensor, length):
        return jnp.moveaxis(value_tensor, 1, 2).reshape(row_total, length, slot_count * HEAD_DIM)

    def as_rows(value_tensor):
        return value_tensor.reshape(row_total, stretch_rows, value_tensor.shape[-1])

    inputs = tokens.astype(jnp.float32)
    normed_one = gather_rows(rms_norm(inputs, norm1_gain).astype(jnp.bfloat16))
    query_proj = plain_dot(normed_one, query_full)
    key_proj = plain_dot(normed_one, key_slots)
    value_low = plain_dot(normed_one, value_slots).astype(jnp.bfloat16)
    query_low = head_path(query_proj, q_gain, own_positions).astype(jnp.bfloat16)
    key_low = (
        head_path(key_proj, k_gain, own_positions)
        .astype(jnp.bfloat16)
        .reshape(flat_rows, slot_count * HEAD_DIM)
    )
    key_all, value_all = (
        lax.all_gather(as_rows(key_low), "ctx", axis=1, tiled=True),
        lax.all_gather(as_rows(value_low), "ctx", axis=1, tiled=True),
    )
    query_slots = by_slot(query_low, stretch_rows)

    def forward_row(row_pieces):
        row_query, row_keys, row_values, row_allowed = row_pieces

        def forward_slot(pieces):
            query, keys, values = pieces
            scores = jnp.where(row_allowed, dot_last(query, keys) * scale, MASKED)
            peak = jnp.max(scores, axis=1, keepdims=True)
            exp_scores = jnp.exp(scores - peak)
            exp_total = jnp.sum(exp_scores, axis=1, keepdims=True)
            probs_low = (exp_scores / exp_total).astype(jnp.bfloat16)
            return (plain_dot(probs_low, values), (peak + jnp.log(exp_total))[:, 0])

        return lax.map(forward_slot, (row_query, row_keys, row_values))

    attended, log_sums = lax.map(
        forward_row,
        (query_slots, by_slot(key_all, row_length), by_slot(value_all, row_length), allowed),
    )
    out_low = by_rows(attended * valid[None, :, None, None], stretch_rows).astype(jnp.bfloat16)

    def out_term(start, count):
        return plain_dot(tp_block(out_low, count, seq_rows), out_full)

    residual = inputs + sum_rows(out_term, local_rows).reshape(row_total, seq_rows, model_width)
    normed_two = gather_rows(rms_norm(residual, norm2_gain).astype(jnp.bfloat16))
    gate = plain_dot(normed_two, gate_full)
    up_proj = plain_dot(normed_two, up_full)
    sigmoid_gate = jax.nn.sigmoid(gate)
    silu_gate = gate * sigmoid_gate
    hidden = (silu_gate * up_proj).astype(jnp.bfloat16)
    hidden_rows = as_rows(hidden)

    def down_term(start, count):
        return plain_dot(tp_block(hidden_rows, count, seq_rows), down_full)

    output = (
        residual + sum_rows(down_term, local_rows).reshape(row_total, seq_rows, model_width)
    ).astype(jnp.bfloat16)
    grad_out_all = gather_rows(cotangent)
    grad_down = dot_first(hidden, grad_out_all)
    grad_hidden = dot_last(grad_out_all, down_full)
    grad_gate_low = (
        grad_hidden * up_proj * sigmoid_gate * (1.0 + gate * (1.0 - sigmoid_gate))
    ).astype(jnp.bfloat16)
    grad_up_low = (grad_hidden * silu_gate).astype(jnp.bfloat16)
    grad_gate_w = dot_first(normed_two, grad_gate_low)
    grad_up_w = dot_first(normed_two, grad_up_low)
    gate_rows = as_rows(grad_gate_low)
    up_rows = as_rows(grad_up_low)

    def ffn_input_term(start, count):
        return dot_last(tp_block(gate_rows, count, seq_rows), gate_full) + dot_last(
            tp_block(up_rows, count, seq_rows), up_full
        )

    grad_normed_two = sum_rows(ffn_input_term, local_rows).reshape(row_total, seq_rows, model_width)
    _, pull_two = jax.vjp(rms_norm, residual, norm2_gain)
    grad_residual_norm, grad_norm_two = pull_two(grad_normed_two)
    grad_residual = cotangent.astype(jnp.float32) + grad_residual_norm
    grad_attn_all = gather_rows(grad_residual.astype(jnp.bfloat16))
    out_flat = out_low.reshape(flat_rows, slot_count * HEAD_DIM)
    grad_out_w = dot_first(out_flat, grad_attn_all)
    grad_out_low = (
        dot_last(grad_attn_all, out_full) * jnp.repeat(valid, HEAD_DIM)[None, :]
    ).astype(jnp.bfloat16)
    key_back, value_back = (
        lax.all_gather(as_rows(key_low), "ctx", axis=1, tiled=True),
        lax.all_gather(as_rows(value_low), "ctx", axis=1, tiled=True),
    )

    def backward_row(row_pieces):
        row_query, row_keys, row_values, row_sums, row_grads, row_allowed = row_pieces

        def backward_slot(pieces):
            query, keys, values, log_sum, grad_slot = pieces
            scores = jnp.where(row_allowed, dot_last(query, keys) * scale, MASKED)
            probs = jnp.exp(scores - log_sum[:, None])
            grad_probs = dot_last(grad_slot, values)
            inner = jnp.sum(grad_probs * probs, axis=1, keepdims=True)
            grad_scores = (probs * (grad_probs - inner)).astype(jnp.bfloat16)
            grad_query = plain_dot(grad_scores, keys) * scale
            grad_keys = dot_first(grad_scores, query) * scale
            grad_values = dot_first(probs.astype(jnp.bfloat16), grad_slot)
            return (grad_query, grad_keys, grad_values)

        return lax.map(backward_slot, (row_query, row_keys, row_values, row_sums, row_grads))

    grad_query, grad_keys, grad_values = lax.map(
        backward_row,
        (
            query_slots,
            by_slot(key_back, row_length),
            by_slot(value_back, row_length),
            log_sums,
            by_slot(grad_out_low, stretch_rows),
            allowed,
        ),
    )
    grad_key_own, grad_value_own = (
        lax.psum_scatter(
            by_rows(grad_keys, row_length).astype(jnp.bfloat16),
            "ctx",
            scatter_dimension=1,
            tiled=True,
        ).astype(jnp.float32),
        lax.psum_scatter(
            by_rows(grad_values, row_length).astype(jnp.bfloat16),
            "ctx",
            scatter_dimension=1,
            tiled=True,
        ).astype(jnp.float32),
    )
    _, pull_query = jax.vjp(
        lambda projected, gain: head_path(projected, gain, own_positions), query_proj, q_gain
    )
    grad_query_proj, grad_q_gain = pull_query(
        jnp.moveaxis(grad_query, 1, 2).reshape(flat_rows, slot_count, HEAD_DIM)
    )
    _, pull_key = jax.vjp(
        lambda projected, gain: head_path(projected, gain, own_positions), key_proj, k_gain
    )
    grad_key_proj, grad_k_gain = pull_key(grad_key_own.reshape(flat_rows, slot_count, HEAD_DIM))
    grad_query_low = grad_query_proj.astype(jnp.bfloat16)
    grad_key_low = grad_key_proj.astype(jnp.bfloat16)
    grad_value_low = grad_value_own.reshape(flat_rows, slot_count * HEAD_DIM).astype(jnp.bfloat16)
    grad_query_w = dot_first(normed_one, grad_query_low)
    select_float = select.astype(jnp.float32)
    grad_key_w = jnp.einsum(
        "dsh,ks->dkh",
        dot_first(normed_one, grad_key_low).reshape(model_width, slot_count, HEAD_DIM),
        select_float,
        precision=lax.Precision.HIGHEST,
    ).reshape(model_width, KVH * HEAD_DIM)
    grad_value_w = jnp.einsum(
        "dsh,ks->dkh",
        dot_first(normed_one, grad_value_low).reshape(model_width, slot_count, HEAD_DIM),
        select_float,
        precision=lax.Precision.HIGHEST,
    ).reshape(model_width, KVH * HEAD_DIM)
    query_rows = as_rows(grad_query_low)
    key_rows = as_rows(grad_key_low)
    value_rows = as_rows(grad_value_low)

    def attn_input_term(start, count):
        return (
            dot_last(tp_block(query_rows, count, seq_rows), query_full)
            + dot_last(tp_block(key_rows, count, seq_rows), key_slots)
            + dot_last(tp_block(value_rows, count, seq_rows), value_slots)
        )

    grad_normed_one = sum_rows(attn_input_term, local_rows).reshape(
        row_total, seq_rows, model_width
    )
    _, pull_one = jax.vjp(rms_norm, inputs, norm1_gain)
    grad_inputs_norm, grad_norm_one = pull_one(grad_normed_one)
    grad_inputs = grad_residual + grad_inputs_norm
    grad_query_w, grad_out_w, grad_gate_w, grad_up_w, grad_down = (
        lax.psum_scatter(
            grad_query_w.astype(jnp.bfloat16), ("dp", "ctx"), scatter_dimension=0, tiled=True
        ).astype(jnp.float32),
        lax.psum_scatter(
            grad_out_w.astype(jnp.bfloat16), ("dp", "ctx"), scatter_dimension=1, tiled=True
        ).astype(jnp.float32),
        lax.psum_scatter(
            grad_gate_w.astype(jnp.bfloat16), ("dp", "ctx"), scatter_dimension=0, tiled=True
        ).astype(jnp.float32),
        lax.psum_scatter(
            grad_up_w.astype(jnp.bfloat16), ("dp", "ctx"), scatter_dimension=0, tiled=True
        ).astype(jnp.float32),
        lax.psum_scatter(
            grad_down.astype(jnp.bfloat16), ("dp", "ctx"), scatter_dimension=1, tiled=True
        ).astype(jnp.float32),
    )
    grad_key_w, grad_value_w, grad_norm_one, grad_norm_two, grad_q_gain, grad_k_gain = lax.psum(
        (grad_key_w, grad_value_w, grad_norm_one, grad_norm_two, grad_q_gain, grad_k_gain),
        ("dp", "ctx", "tp"),
    )
    return (
        output,
        grad_inputs,
        grad_norm_one,
        grad_norm_two,
        grad_q_gain,
        grad_k_gain,
        grad_query_w,
        grad_key_w,
        grad_value_w,
        grad_out_w,
        grad_gate_w,
        grad_up_w,
        grad_down,
    )


def solution(mesh):
    return jax.shard_map(
        body,
        mesh=mesh,
        in_specs=(
            P("dp", ("ctx", "tp"), None),
            P("dp", ("ctx", "tp"), None),
            P("dp", None),
            P(),
            P(),
            P(),
            P(),
            P(),
            P(("dp", "ctx"), "tp"),
            P(),
            P(),
            P("tp", ("dp", "ctx")),
            P(("dp", "ctx"), "tp"),
            P(("dp", "ctx"), "tp"),
            P("tp", ("dp", "ctx")),
        ),
        out_specs=(
            P("dp", ("ctx", "tp"), None),
            P("dp", ("ctx", "tp"), None),
            P(),
            P(),
            P(),
            P(),
            P(("dp", "ctx"), "tp"),
            P(),
            P(),
            P("tp", ("dp", "ctx")),
            P(("dp", "ctx"), "tp"),
            P(("dp", "ctx"), "tp"),
            P("tp", ("dp", "ctx")),
        ),
        check_vma=False,
    )
```

profile of v0, /device:TPU:0, one launch (start us, length us, event | category | flops | bytes accessed | tf_op | source)
XLA Modules:
  0.0 3367.5 jit_solution(612909178825626275)
XLA Ops:
  20.3 40.3 %all-gather.12.cloned.1.call-done = bf16[2,384,2048]{2,1,0:T(8,128)(2,1)} async-done(((bf16[2,192,2048]{2,1,0:T(8,128)(2,1)}), bf16[2,384,2048]{2,1,0:T(8,128)(2,1)}) %all-gather.12.cloned.1.call-update) | async-done | bytes 3145744 | tf_op jit(solution)/shard_map/all_gather | solution.py:60
  77.1 30.9 all-gather.14.cloned.1.call-done
  136.9 61.6 %all-gather.18.cloned.1.call-done = bf16[2,1536,768]{1,2,0:T(8,128)(2,1)} async-done(((bf16[2,384,768]{1,2,0:T(8,128)(2,1)}), bf16[2,1536,768]{1,2,0:T(8,128)(2,1)}) %all-gather.18.cloned.1.call-update) | async-done | bytes 4718608 | tf_op jit(solution)/shard_map/all_gather | solution.py:196
  198.5 9.7 copy.105
  208.1 80.3 %all-gather.16.cloned.1.call-done = bf16[2,1536,768]{1,2,0:T(8,128)(2,1)} async-done(((bf16[2,384,768]{1,2,0:T(8,128)(2,1)}), bf16[2,1536,768]{1,2,0:T(8,128)(2,1)}) %all-gather.16.cloned.1.call-update) | async-done | bytes 4718608 | tf_op jit(solution)/shard_map/all_gather | solution.py:195
  288.4 9.7 copy.104
  299.8 134.2 %while.53 = (s32[]{:T(128)}, f32[2,12,384,64]{2,3,1,0:T(8,128)}, f32[2,12,384]{2,1,0:T(8,128)S(1)}, bf16[2,12,384,64]{3,2,1,0:T(8,128)(2,1)}, bf16[2,12,1536,64]...) while((s32[]{:T(128)}, f32[2,12,384,64]{2,3,1,0:T(8,128)}, ...), condition=%wide.region_10.11_spmd, body=%wide.region_5.10_spmd.sunk | while | flops 155713152 | bytes 32313720 | solution.py:214
  302.2 8.4 dynamic-slice_bitcast_fusion.18
  310.6 53.8 %while.56 = (s32[]{:T(128)}, f32[12,384,64]{1,2,0:T(8,128)}, f32[12,384]{1,0:T(8,128)S(1)}, bf16[12,384,64]{2,1,0:T(8,128)(2,1)S(1)}, bf16[12,1536,64]{2,1,0:T(8...) while((s32[]{:T(128)}, f32[12,384,64]{1,2,0:T(8,128)}, ...), condition=%wide.region_9.9_spmd, body=%wide.region_6.8_spmd.sunk | while | flops 155713152 | bytes 8671337 | solution.py:212
  369.4 8.4 dynamic-slice_bitcast_fusion.18
  377.7 53.7 %while.56 = (s32[]{:T(128)}, f32[12,384,64]{1,2,0:T(8,128)}, f32[12,384]{1,0:T(8,128)S(1)}, bf16[12,384,64]{2,1,0:T(8,128)(2,1)S(1)}, bf16[12,1536,64]{2,1,0:T(8...) while((s32[]{:T(128)}, f32[12,384,64]{1,2,0:T(8,128)}, ...), condition=%wide.region_9.9_spmd, body=%wide.region_6.8_spmd.sunk | while | flops 155713152 | bytes 8671337 | solution.py:212
  448.3 75.6 %reduce-scatter.20.cloned.1.call-done = f32[384,2048]{1,0:T(8,128)} async-done(((f32[768,2048]{1,0:T(8,128)}), f32[384,2048]{1,0:T(8,128)}) %reduce-scatter.20.cloned.1.call-update) | async-done | bytes 3145744 | tf_op jit(solution)/shard_map/reduce_scatter | solution.py:65
  532.5 42.0 %all-gather.22.cloned.1.call-done = bf16[2,384,2048]{2,1,0:T(8,128)(2,1)} async-done(((bf16[2,192,2048]{2,1,0:T(8,128)(2,1)}), bf16[2,384,2048]{2,1,0:T(8,128)(2,1)}) %all-gather.22.cloned.1.call-update) | async-done | bytes 3145744 | tf_op jit(solution)/shard_map/all_gather | solution.py:60
  574.5 129.4 %all-gather.26.cloned.1.call-done = bf16[2048,4096]{1,0:T(8,128)(2,1)} async-done(((bf16[128,4096]{1,0:T(8,128)(2,1)}), bf16[2048,4096]{1,0:T(8,128)(2,1)}) %all-gather.26.cloned.1.call-update) | async-done | bytes 16777232 | tf_op jit(solution)/shard_map/all_gather | solution.py:150
  703.9 20.2 fusion.93
  724.1 107.4 %all-gather.24.cloned.1.call-done = bf16[2048,4096]{1,0:T(8,128)(2,1)} async-done(((bf16[128,4096]{1,0:T(8,128)(2,1)}), bf16[2048,4096]{1,0:T(8,128)(2,1)}) %all-gather.24.cloned.1.call-update) | async-done | bytes 16777232 | tf_op jit(solution)/shard_map/all_gather | solution.py:149
  831.5 20.2 fusion.92
  851.7 24.4 all-gather.30.cloned.1.call-done
  876.1 132.7 %all-gather.28.cloned.1.call-done = bf16[4096,2048]{1,0:T(8,128)(2,1)} async-done(((bf16[4096,128]{1,0:T(8,128)(2,1)}), bf16[4096,2048]{1,0:T(8,128)(2,1)}) %all-gather.28.cloned.1.call-update) | async-done | bytes 16777232 | tf_op jit(solution)/shard_map/all_gather | solution.py:151
  1008.7 29.0 multiply_convert_fusion.1
  1045.4 18.4 fusion.95
  1063.8 21.3 convolution_add_fusion
  1085.2 75.3 %reduce-scatter.24.cloned.1.call-done = f32[384,2048]{1,0:T(8,128)} async-done(((f32[768,2048]{1,0:T(8,128)}), f32[384,2048]{1,0:T(8,128)}) %reduce-scatter.24.cloned.1.call-update) | async-done | bytes 3145744 | tf_op jit(solution)/shard_map/reduce_scatter | solution.py:65
  1167.7 44.9 %all-gather.32.cloned.1.call-done = bf16[2,384,2048]{2,1,0:T(8,128)(2,1)} async-done(((bf16[2,192,2048]{2,1,0:T(8,128)(2,1)}), bf16[2,384,2048]{2,1,0:T(8,128)(2,1)}) %all-gather.32.cloned.1.call-update) | async-done | bytes 3145744 | tf_op jit(solution)/shard_map/all_gather | solution.py:60
  1221.7 258.5 %while.55 = (s32[]{:T(128)}, f32[2,12,384,64]{2,3,1,0:T(8,128)}, bf16[2,12,1536,64]{2,3,1,0:T(8,128)(2,1)}, bf16[2,12,1536,64]{2,3,1,0:T(8,128)(2,1)}, bf16[2,12...) while((s32[]{:T(128)}, f32[2,12,384,64]{2,3,1,0:T(8,128)}, ...), condition=%wide.region_21.22_spmd, body=%wide.region_17.21_spmd.sunk | while | flops 382918272 | bytes 75056560 | solution.py:287
  1238.5 105.7 %while.57 = (s32[]{:T(128)}, f32[12,384,64]{1,2,0:T(8,128)}, bf16[12,1536,64]{1,2,0:T(8,128)(2,1)}, bf16[12,1536,64]{1,2,0:T(8,128)(2,1)}, bf16[12,384,64]{2,1,0...) while((s32[]{:T(128)}, f32[12,384,64]{1,2,0:T(8,128)}, ...), condition=%wide.region_20.20_spmd, body=%wide.region_18.19_spmd.sunk | while | flops 382918272 | bytes 20755576 | solution.py:285
  1367.8 105.7 %while.57 = (s32[]{:T(128)}, f32[12,384,64]{1,2,0:T(8,128)}, bf16[12,1536,64]{1,2,0:T(8,128)(2,1)}, bf16[12,1536,64]{1,2,0:T(8,128)(2,1)}, bf16[12,384,64]{2,1,0...) while((s32[]{:T(128)}, f32[12,384,64]{1,2,0:T(8,128)}, ...), condition=%wide.region_20.20_spmd, body=%wide.region_18.19_spmd.sunk | while | flops 382918272 | bytes 20755576 | solution.py:285
  1480.2 9.3 copy.116
  1489.5 210.1 %copy.126 = bf16[2,1536,768]{0,2,1:T(8,128)(2,1)} copy(bf16[2,1536,768]{1,0,2:T(2,128)(2,1)} %bitcast.319) | data formatting | bytes 9437184
  1699.6 484.8 %reshape.444 = bf16[1536,1536]{1,0:T(8,128)(2,1)} reshape(bf16[1536,768,2]{2,1,0:T(8,128)(2,1)} %bitcast.94) | data formatting | bytes 9437184
  2184.4 12.6 copy.128
  2214.6 19.7 convolution_convert_fusion
  2234.3 21.4 copy.132
  2255.8 19.8 convolution_convert_fusion.1
  2275.7 20.0 convolution_convert_fusion.2
  2299.2 164.2 %reshape.445 = bf16[384,768,2]{2,1,0:T(8,128)(2,1)} reshape(bf16[384,1536]{1,0:T(8,128)(2,1)} %reduce-scatter.34.cloned.1.call-done) | data formatting | bytes 2359296
  2463.5 68.4 %copy.127 = bf16[2,384,768]{1,0,2:T(2,128)(2,1)S(1)} copy(bf16[2,384,768]{0,2,1:T(8,128)(2,1)} %bitcast.95) | data formatting | bytes 2359296
  2587.9 18.7 fusion.94
  2613.1 6.5 fusion.53
  2626.6 6.5 fusion.50
  2641.5 149.6 %reduce-scatter.32.cloned.1.call-done = bf16[128,4096]{1,0:T(8,128)(2,1)} async-done(((bf16[2048,4096]{1,0:T(8,128)(2,1)}), bf16[128,4096]{1,0:T(8,128)(2,1)}) %reduce-scatter.32.cloned.1.call-update) | async-done | bytes 1048592 | tf_op jit(solution)/shard_map/reduce_scatter | solution.py:366
  2793.9 179.0 %reduce-scatter.30.cloned.1.call-done = bf16[128,4096]{1,0:T(8,128)(2,1)} async-done(((bf16[2048,4096]{1,0:T(8,128)(2,1)}), bf16[128,4096]{1,0:T(8,128)(2,1)}) %reduce-scatter.30.cloned.1.call-update) | async-done | bytes 1048592 | tf_op jit(solution)/shard_map/reduce_scatter | solution.py:363
  2975.6 66.1 %reduce-scatter.28.cloned.1.call-done = bf16[128,768]{1,0:T(8,128)(2,1)} async-done(((bf16[2048,768]{1,0:T(8,128)(2,1)}), bf16[128,768]{1,0:T(8,128)(2,1)}) %reduce-scatter.28.cloned.1.call-update) | async-done | bytes 196624 | tf_op jit(solution)/shard_map/reduce_scatter | solution.py:357
  3043.4 76.7 %reduce-scatter.26.cloned.1.call-done = f32[384,2048]{1,0:T(8,128)} async-done(((f32[768,2048]{1,0:T(8,128)}), f32[384,2048]{1,0:T(8,128)}) %reduce-scatter.26.cloned.1.call-update) | async-done | bytes 3145744 | tf_op jit(solution)/shard_map/reduce_scatter | solution.py:65
  3123.0 40.2 %all-reduce.4 = (f32[2048]{0:T(1024)}, f32[2048]{0:T(1024)}, f32[64]{0:T(128)}, f32[64]{0:T(128)}) all-reduce(f32[2048]{0:T(1024)S(1)} %get-tuple-element.259, f32[2048]{0:T(1024)S(1)} %copy-done.51, f32[64]{0:T(128)S(1)} %get-tuple-element.257, f32[64]{0:T(128)S(1)} %get-tuple-element.255), channel_id=1, replica_groups=mesh['dp'=4,'ctx'=4,'tp'=2] {'dp','ctx','tp'}, use_global_device_ids=true, to_apply=%region_29.30 | all-reduce | flops 4224 | bytes 33792 | tf_op jit(solution)/shard_map/psum | solution.py:373
  3163.2 37.6 %reduce-scatter.22.cloned.1.call-done = f32[384,2048]{1,0:T(8,128)} async-done(((f32[768,2048]{1,0:T(8,128)}), f32[384,2048]{1,0:T(8,128)}) %reduce-scatter.22.cloned.1.call-update) | async-done | bytes 3145744 | tf_op jit(solution)/shard_map/reduce_scatter | solution.py:65
  3200.8 7.7 fusion.59
  3208.4 146.9 %all-reduce.8.cloned.1.call-done = (f32[2048,320]{0,1:T(8,128)}, f32[2048,320]{0,1:T(8,128)}) async-done(((f32[2048,320]{0,1:T(8,128)}, f32[2048,320]{0,1:T(8,128)}), (f32[2048,320]{0,1:T(8,128)}, f32[2048,320]{0,1:T(8,128)})) %all-reduce.8.cloned.1.call-update) | async-done | bytes 5242896 | tf_op jit(solution)/shard_map/psum | solution.py:373
  (664 shorter events, 595.3 us)
Async XLA Ops:
  7.2 7.6 copy-start
  7.2 53.3 %all-gather.12.cloned.1.call-start = ((), (), s32[]{:S(2)}) async-start(), calls=%async_computation.11 | async-start | bytes 4718592 | tf_op jit(solution)/shard_map/all_gather | solution.py:60
  12.7 95.4 %all-gather.14.cloned.1.call-start = ((), (), s32[]{:S(2)}) async-start(), calls=%async_computation.12 | async-start | bytes 3342336 | tf_op jit(solution)/shard_map/all_gather | solution.py:147
  13.5 185.0 %all-gather.18.cloned.1.call-start = ((), (), s32[]{:S(2)}) async-start(), calls=%async_computation.14 | async-start | bytes 5898240 | tf_op jit(solution)/shard_map/all_gather | solution.py:196
  14.8 54.0 %copy-start.60 = (s32[12]{0:T(128)}, s32[12]{0:T(128)S(1)}, u32[]{:S(2)}) copy-start(s32[12]{0:T(128)S(1)} %fusion.89) | copy-start | bytes 148
  67.5 220.9 %all-gather.16.cloned.1.call-start = ((), (), s32[]{:S(2)}) async-start(), calls=%async_computation.13 | async-start | bytes 5898240 | tf_op jit(solution)/shard_map/all_gather | solution.py:195
  73.0 46.9 %copy-start.30 = (f32[768,32]{0,1:T(8,128)}, f32[768,32]{0,1:T(8,128)S(1)}, u32[]{:S(2)}) copy-start(f32[768,32]{0,1:T(8,128)S(1)} %get-tuple-element.371) | copy-start | bytes 294916
  73.0 46.9 %copy-start.32 = (f32[768,32]{0,1:T(8,128)}, f32[768,32]{0,1:T(8,128)S(1)}, u32[]{:S(2)}) copy-start(f32[768,32]{0,1:T(8,128)S(1)} %get-tuple-element.372) | copy-start | bytes 294916
  77.1 35.6 %copy-start.40 = (f32[768,12]{0,1:T(8,128)}, f32[768,12]{0,1:T(8,128)S(1)}, u32[]{:S(2)}) copy-start(f32[768,12]{0,1:T(8,128)S(1)} %get-tuple-element.373) | copy-start | bytes 110596
  77.1 41.4 %copy-start.34 = (f32[768,12]{0,1:T(8,128)}, f32[768,12]{0,1:T(8,128)S(1)}, u32[]{:S(2)}) copy-start(f32[768,12]{0,1:T(8,128)S(1)} %fusion.72) | copy-start | bytes 110596
  112.7 5.8 copy-start.62
  112.7 5.8 copy-start.64
  123.1 318.7 %all-gather.20.cloned.1.call-start = ((), (), s32[]{:S(2)}) async-start(), calls=%async_computation.15 | async-start | bytes 3342336 | tf_op jit(solution)/shard_map/all_gather | solution.py:148
  123.7 400.2 %reduce-scatter.20.cloned.1.call-start = ((), (), s32[]{:S(2)}) async-start(), calls=%async_computation.16 | async-start | bytes 9437184 | tf_op jit(solution)/shard_map/reduce_scatter | solution.py:65
  299.8 134.2 %copy-start.66 = (f32[12]{0:T(128)S(1)}, f32[12]{0:T(128)}, u32[]{:S(2)}) copy-start(f32[12]{0:T(128)} %compare_convert_fusion.2) | copy-start | bytes 148
  434.0 14.2 copy-start.8
  448.2 75.7 %copy-start.10 = (bf16[2,192,2048]{2,1,0:T(8,128)(2,1)S(1)}, bf16[2,192,2048]{2,1,0:T(8,128)(2,1)}, u32[]{:S(2)}) copy-start(bf16[2,192,2048]{2,1,0:T(8,128)(2,1)} %param.23) | copy-start | bytes 4718596
  448.2 126.3 %all-gather.22.cloned.1.call-start = ((), (), s32[]{:S(2)}) async-start(), calls=%async_computation.17 | async-start | bytes 4718592 | tf_op jit(solution)/shard_map/all_gather | solution.py:60
  529.4 174.5 %all-gather.26.cloned.1.call-start = ((), (), s32[]{:S(2)}) async-start(), calls=%async_computation.19 | async-start | bytes 17825792 | tf_op jit(solution)/shard_map/all_gather | solution.py:150
  530.2 301.3 %all-gather.24.cloned.1.call-start = ((), (), s32[]{:S(2)}) async-start(), calls=%async_computation.18 | async-start | bytes 17825792 | tf_op jit(solution)/shard_map/all_gather | solution.py:149
  530.9 345.1 %all-gather.30.cloned.1.call-start = ((), (), s32[]{:S(2)}) async-start(), calls=%async_computation.22 | async-start | bytes 4718592 | tf_op jit(solution)/shard_map/all_gather | solution.py:60
  531.5 477.2 %all-gather.28.cloned.1.call-start = ((), (), s32[]{:S(2)}) async-start(), calls=%async_computation.20 | async-start | bytes 17825792 | tf_op jit(solution)/shard_map/all_gather | solution.py:151
  532.3 628.3 %reduce-scatter.24.cloned.1.call-start = ((), (), s32[]{:S(2)}) async-start(), calls=%async_computation.23 | async-start | bytes 9437184 | tf_op jit(solution)/shard_map/reduce_scatter | solution.py:65
  1085.1 75.4 %copy-start.45 = (f32[2048]{0:T(1024)S(1)}, f32[2048]{0:T(1024)}, u32[]{:S(2)}) copy-start(f32[2048]{0:T(1024)} %param.28) | copy-start | bytes 24580
  1085.1 75.4 %copy-start.49 = (f32[2,192]{1,0:T(2,128)S(1)}, f32[2,192]{1,0:T(2,128)}, u32[]{:S(2)}) copy-start(f32[2,192]{1,0:T(2,128)} %copy-done.48) | copy-start | bytes 4612
  1085.1 79.8 %copy-start.17 = (bf16[2,192,2048]{2,1,0:T(8,128)(2,1)S(1)}, bf16[2,192,2048]{2,1,0:T(8,128)(2,1)}, u32[]{:S(2)}) copy-start(bf16[2,192,2048]{2,1,0:T(8,128)(2,1)} %param.24) | copy-start | bytes 4718596
  1085.1 127.4 %all-gather.32.cloned.1.call-start = ((), (), s32[]{:S(2)}) async-start(), calls=%async_computation.24 | async-start | bytes 4718592 | tf_op jit(solution)/shard_map/all_gather | solution.py:60
  1167.4 1131.8 %reduce-scatter.34.cloned.1.call-start = ((), (), s32[]{:S(2)}) async-start(), calls=%async_computation.29 | async-start | bytes 5898240
  1229.2 6.8 copy-start.2
  1358.5 6.8 copy-start.2
  2184.4 365.8 %reduce-scatter.36.cloned.1.call-start = ((), (), s32[]{:S(2)}) async-start(), calls=%async_computation.30 | async-start | bytes 5898240
  2202.6 433.6 %reduce-scatter.38.cloned.1.call-start = ((), (), s32[]{:S(2)}) async-start(), calls=%async_computation.31 | async-start | bytes 3342336
  2214.5 423.5 %reduce-scatter.40.cloned.1.call-start = ((), (), s32[]{:S(2)}) async-start(), calls=%async_computation.32 | async-start | bytes 17825792
  2255.7 535.4 %reduce-scatter.32.cloned.1.call-start = ((), (), s32[]{:S(2)}) async-start(), calls=%async_computation.28 | async-start | bytes 17825792 | tf_op jit(solution)/shard_map/reduce_scatter | solution.py:366
  2275.6 697.2 %reduce-scatter.30.cloned.1.call-start = ((), (), s32[]{:S(2)}) async-start(), calls=%async_computation.27 | async-start | bytes 17825792 | tf_op jit(solution)/shard_map/reduce_scatter | solution.py:363
  2295.8 745.9 %reduce-scatter.28.cloned.1.call-start = ((), (), s32[]{:S(2)}) async-start(), calls=%async_computation.26 | async-start | bytes 3342336 | tf_op jit(solution)/shard_map/reduce_scatter | solution.py:357
  2544.3 575.7 %reduce-scatter.26.cloned.1.call-start = ((), (), s32[]{:S(2)}) async-start(), calls=%async_computation.25 | async-start | bytes 9437184 | tf_op jit(solution)/shard_map/reduce_scatter | solution.py:65
  2556.3 5.9 copy-start.35
  2556.3 5.9 copy-start.65
  2584.6 616.2 %reduce-scatter.22.cloned.1.call-start = ((), (), s32[]{:S(2)}) async-start(), calls=%async_computation.21 | async-start | bytes 9437184 | tf_op jit(solution)/shard_map/reduce_scatter | solution.py:65
  2606.6 748.7 %all-reduce.8.cloned.1.call-start = ((), (), s32[]{:S(2)}) async-start(), calls=%async_computation.33 | async-start | bytes 10485760 | tf_op jit(solution)/shard_map/psum | solution.py:373
  2793.9 326.2 %copy-start.11 = (bf16[2,192,2048]{2,1,0:T(8,128)(2,1)S(1)}, bf16[2,192,2048]{2,1,0:T(8,128)(2,1)}, u32[]{:S(2)}) copy-start(bf16[2,192,2048]{2,1,0:T(8,128)(2,1)} %param.23) | copy-start | bytes 4718596
  2793.9 326.2 %copy-start.47 = (f32[2048]{0:T(1024)S(1)}, f32[2048]{0:T(1024)}, u32[]{:S(2)}) copy-start(f32[2048]{0:T(1024)} %param.27) | copy-start | bytes 24580
  2793.9 326.2 %copy-start.53 = (f32[2,192]{1,0:T(2,128)S(1)}, f32[2,192]{1,0:T(2,128)}, u32[]{:S(2)}) copy-start(f32[2,192]{1,0:T(2,128)} %copy-done.52) | copy-start | bytes 4612
  3120.1 43.1 %copy-start.55 = (f32[2,192]{1,0:T(2,128)S(1)}, f32[2,192]{1,0:T(2,128)}, u32[]{:S(2)}) copy-start(f32[2,192]{1,0:T(2,128)} %copy-done.54) | copy-start | bytes 4612
  3120.1 80.7 %copy-start.46 = (f32[2048]{0:T(1024)S(1)}, f32[2048]{0:T(1024)}, u32[]{:S(2)}) copy-start(f32[2048]{0:T(1024)} %param.28) | copy-start | bytes 24580
  3120.1 80.7 %copy-start.50 = (f32[2,192]{1,0:T(2,128)S(1)}, f32[2,192]{1,0:T(2,128)}, u32[]{:S(2)}) copy-start(f32[2,192]{1,0:T(2,128)} %copy-done.48) | copy-start | bytes 4612
  3120.1 80.7 %copy-start.59 = (f32[2,192]{1,0:T(2,128)S(1)}, f32[2,192]{1,0:T(2,128)}, u32[]{:S(2)}) copy-start(f32[2,192]{1,0:T(2,128)} %copy-done.58) | copy-start | bytes 4612
  (56 other events, 156.5 us)
Sparse Core Ops, SparseCore 0:
  12.8 47.6 all-gather.11
  62.8 45.2 all-gather.13
  110.2 88.1 all-gather.17
  200.5 87.8 all-gather.15
  290.3 46.6 all-gather.19
  448.3 75.5 reduce-scatter.19
  529.6 44.9 all-gather.21
  577.0 126.8 all-gather.25
  706.4 125.0 all-gather.23
  832.9 43.0 all-gather.29
  878.4 130.3 all-gather.27
  1085.3 75.2 reduce-scatter.23
  1167.6 44.9 all-gather.31
  2184.5 85.2 reduce-scatter.33
  2272.0 85.7 reduce-scatter.35
  2361.4 66.7 reduce-scatter.37
  2432.2 177.4 reduce-scatter.39
  2613.6 177.4 reduce-scatter.31
  2795.2 177.5 reduce-scatter.29
  2976.5 65.1 reduce-scatter.27
  3044.0 76.0 reduce-scatter.25
  3122.5 78.2 reduce-scatter.21
  3207.7 147.5 all-reduce.7
where the time goes:
time: 3390 us; the launch traced here: 3370 us
  waiting for transfers between devices  1500 us (44%)
  local copies, waits for them, and re-layouts  1170 us (35%)
  matrix products  557 us (16%)
  other arithmetic  78.4 us (2%)
  blocking collectives  40.2 us (1%)
    unnamed x159, local copies, waits for them, and re-layouts  995 us
    reduce_scatter x4, waiting for transfers between devices, sum_rows(): lax.psum_scatter(term_fn(jnp.int32(0), row_count * lax.axis_size('tp')),...  265 us
    dot_general x79, matrix products, dot_last(): lax.dot_general(left, right, (((1,), (1,)), ((), ())), preferred_element_...  205 us
    dot_general x55, matrix products, plain_dot(): return jnp.dot(left, right, preferred_element_type=jnp.float32)  188 us
    reduce_scatter x1, waiting for transfers between devices, body(): lax.psum_scatter(grad_gate_w.astype(jnp.bfloat16), ('dp', 'ctx'), scatter...  179 us
    all_gather x4, waiting for transfers between devices, gather_rows(): gathered = lax.all_gather(value_tensor, 'tp', axis=1, tiled=True)  152 us
    reduce_scatter x1, waiting for transfers between devices, body(): lax.psum_scatter(grad_up_w.astype(jnp.bfloat16), ('dp', 'ctx'), scatter_d...  150 us
    dot_general x55, matrix products, dot_first(): lax.dot_general(left, right, (((0,), (0,)), ((), ())), preferred_element_...  147 us
  transfers between devices with their start and end apart: 23, of which 18 were waited for; matrix products, arithmetic and copies ran while one was open for 21% of the time, Pallas kernels for 0%

commit v1 on v0

--- a/solution.py
+++ b/solution.py
@@ -371,8 +371,11 @@
         ).astype(jnp.float32),
     )
     grad_key_w, grad_value_w, grad_norm_one, grad_norm_two, grad_q_gain, grad_k_gain = lax.psum(
-        (grad_key_w, grad_value_w, grad_norm_one, grad_norm_two, grad_q_gain, grad_k_gain),
-        ("dp", "ctx", "tp"),
+        lax.psum(
+            (grad_key_w, grad_value_w, grad_norm_one, grad_norm_two, grad_q_gain, grad_k_gain),
+            ("ctx", "tp"),
+        ),
+        "dp",
     )
     return (
         output,

time: 3390 us -> 3710 us (1.094)
  waiting for transfers between devices: 1500 us -> 1820 us
    unnamed x27 -> x28, waiting for transfers between devices: 4.13 us -> 317 us
    psum x1, waiting for transfers between devices: 147 us -> 32.1 us  [body(): lax.psum((grad_key_w, grad_value_w, grad_norm_one, grad_norm_two, grad_q_...]
    psum x0 -> x1, waiting for transfers between devices: none -> 97.3 us  [body(): lax.psum(lax.psum((grad_key_w, grad_value_w, grad_norm_one, grad_norm_two...]
  transfers between devices with their start and end apart: 23 -> 24, of which waited for: 18 -> 22; matrix products, arithmetic and copies ran while one was open for 21% -> 31% of each run, Pallas kernels for 0% -> 0%
where the time goes in v1:
time: 3710 us; the launch traced here: 3680 us
  waiting for transfers between devices  1820 us (49%)
  local copies, waits for them, and re-layouts  1160 us (31%)
  matrix products  557 us (15%)
  other arithmetic  77.5 us (2%)
  blocking collectives  48.6 us (1%)
    unnamed x159, local copies, waits for them, and re-layouts  991 us
    unnamed x28, waiting for transfers between devices  317 us
    reduce_scatter x4, waiting for transfers between devices, sum_rows(): lax.psum_scatter(term_fn(jnp.int32(0), row_count * lax.axis_size('tp')),...  257 us
    dot_general x79, matrix products, dot_last(): lax.dot_general(left, right, (((1,), (1,)), ((), ())), preferred_element_...  205 us
    dot_general x55, matrix products, plain_dot(): return jnp.dot(left, right, preferred_element_type=jnp.float32)  188 us
    reduce_scatter x1, waiting for transfers between devices, body(): lax.psum_scatter(grad_gate_w.astype(jnp.bfloat16), ('dp', 'ctx'), scatter...  179 us
    reduce_scatter x1, waiting for transfers between devices, body(): lax.psum_scatter(grad_up_w.astype(jnp.bfloat16), ('dp', 'ctx'), scatter_d...  179 us
    all_gather x4, waiting for transfers between devices, gather_rows(): gathered = lax.all_gather(value_tensor, 'tp', axis=1, tiled=True)  151 us
  transfers between devices with their start and end apart: 24, of which 22 were waited for; matrix products, arithmetic and copies ran while one was open for 31% of the time, Pallas kernels for 0%

profile of v1, /device:TPU:0, one launch (start us, length us, event | category | flops | bytes accessed | tf_op | source)
XLA Modules:
  0.0 3684.1 jit_solution(2703816156928916872)
XLA Ops:
  20.2 40.3 %all-gather.12.cloned.1.call-done = bf16[2,384,2048]{2,1,0:T(8,128)(2,1)} async-done(((bf16[2,192,2048]{2,1,0:T(8,128)(2,1)}), bf16[2,384,2048]{2,1,0:T(8,128)(2,1)}) %all-gather.12.cloned.1.call-update) | async-done | bytes 3145744 | tf_op jit(solution)/shard_map/all_gather | solution.py:60
  76.8 31.2 all-gather.14.cloned.1.call-done
  136.6 61.8 %all-gather.18.cloned.1.call-done = bf16[2,1536,768]{1,2,0:T(8,128)(2,1)} async-done(((bf16[2,384,768]{1,2,0:T(8,128)(2,1)}), bf16[2,1536,768]{1,2,0:T(8,128)(2,1)}) %all-gather.18.cloned.1.call-update) | async-done | bytes 4718608 | tf_op jit(solution)/shard_map/all_gather | solution.py:196
  198.4 9.7 copy.105
  208.1 80.3 %all-gather.16.cloned.1.call-done = bf16[2,1536,768]{1,2,0:T(8,128)(2,1)} async-done(((bf16[2,384,768]{1,2,0:T(8,128)(2,1)}), bf16[2,1536,768]{1,2,0:T(8,128)(2,1)}) %all-gather.16.cloned.1.call-update) | async-done | bytes 4718608 | tf_op jit(solution)/shard_map/all_gather | solution.py:195
  288.3 9.7 copy.104
  299.7 134.2 %while.53 = (s32[]{:T(128)}, f32[2,12,384,64]{2,3,1,0:T(8,128)}, f32[2,12,384]{2,1,0:T(8,128)S(1)}, bf16[2,12,384,64]{3,2,1,0:T(8,128)(2,1)}, bf16[2,12,1536,64]...) while((s32[]{:T(128)}, f32[2,12,384,64]{2,3,1,0:T(8,128)}, ...), condition=%wide.region_10.11_spmd, body=%wide.region_5.10_spmd.sunk | while | flops 155713152 | bytes 32313720 | solution.py:214
  310.5 53.8 %while.56 = (s32[]{:T(128)}, f32[12,384,64]{1,2,0:T(8,128)}, f32[12,384]{1,0:T(8,128)S(1)}, bf16[12,384,64]{2,1,0:T(8,128)(2,1)S(1)}, bf16[12,1536,64]{2,1,0:T(8...) while((s32[]{:T(128)}, f32[12,384,64]{1,2,0:T(8,128)}, ...), condition=%wide.region_9.9_spmd, body=%wide.region_6.8_spmd.sunk | while | flops 155713152 | bytes 8671337 | solution.py:212
  377.7 53.7 %while.56 = (s32[]{:T(128)}, f32[12,384,64]{1,2,0:T(8,128)}, f32[12,384]{1,0:T(8,128)S(1)}, bf16[12,384,64]{2,1,0:T(8,128)(2,1)S(1)}, bf16[12,1536,64]{2,1,0:T(8...) while((s32[]{:T(128)}, f32[12,384,64]{1,2,0:T(8,128)}, ...), condition=%wide.region_9.9_spmd, body=%wide.region_6.8_spmd.sunk | while | flops 155713152 | bytes 8671337 | solution.py:212
  448.2 75.6 %reduce-scatter.20.cloned.1.call-done = f32[384,2048]{1,0:T(8,128)} async-done(((f32[768,2048]{1,0:T(8,128)}), f32[384,2048]{1,0:T(8,128)}) %reduce-scatter.20.cloned.1.call-update) | async-done | bytes 3145744 | tf_op jit(solution)/shard_map/reduce_scatter | solution.py:65
  532.6 41.8 %all-gather.22.cloned.1.call-done = bf16[2,384,2048]{2,1,0:T(8,128)(2,1)} async-done(((bf16[2,192,2048]{2,1,0:T(8,128)(2,1)}), bf16[2,384,2048]{2,1,0:T(8,128)(2,1)}) %all-gather.22.cloned.1.call-update) | async-done | bytes 3145744 | tf_op jit(solution)/shard_map/all_gather | solution.py:60
  574.4 129.4 %all-gather.26.cloned.1.call-done = bf16[2048,4096]{1,0:T(8,128)(2,1)} async-done(((bf16[128,4096]{1,0:T(8,128)(2,1)}), bf16[2048,4096]{1,0:T(8,128)(2,1)}) %all-gather.26.cloned.1.call-update) | async-done | bytes 16777232 | tf_op jit(solution)/shard_map/all_gather | solution.py:150
  703.8 20.2 fusion.93
  724.0 107.3 %all-gather.24.cloned.1.call-done = bf16[2048,4096]{1,0:T(8,128)(2,1)} async-done(((bf16[128,4096]{1,0:T(8,128)(2,1)}), bf16[2048,4096]{1,0:T(8,128)(2,1)}) %all-gather.24.cloned.1.call-update) | async-done | bytes 16777232 | tf_op jit(solution)/shard_map/all_gather | solution.py:149
  831.3 20.2 fusion.92
  851.5 24.4 all-gather.30.cloned.1.call-done
  875.9 132.7 %all-gather.28.cloned.1.call-done = bf16[4096,2048]{1,0:T(8,128)(2,1)} async-done(((bf16[4096,128]{1,0:T(8,128)(2,1)}), bf16[4096,2048]{1,0:T(8,128)(2,1)}) %all-gather.28.cloned.1.call-update) | async-done | bytes 16777232 | tf_op jit(solution)/shard_map/all_gather | solution.py:151
  1008.6 28.8 multiply_convert_fusion.1
  1045.1 18.4 fusion.95
  1063.5 21.5 convolution_add_fusion
  1085.1 75.3 %reduce-scatter.24.cloned.1.call-done = f32[384,2048]{1,0:T(8,128)} async-done(((f32[768,2048]{1,0:T(8,128)}), f32[384,2048]{1,0:T(8,128)}) %reduce-scatter.24.cloned.1.call-update) | async-done | bytes 3145744 | tf_op jit(solution)/shard_map/reduce_scatter | solution.py:65
  1167.5 44.9 %all-gather.32.cloned.1.call-done = bf16[2,384,2048]{2,1,0:T(8,128)(2,1)} async-done(((bf16[2,192,2048]{2,1,0:T(8,128)(2,1)}), bf16[2,384,2048]{2,1,0:T(8,128)(2,1)}) %all-gather.32.cloned.1.call-update) | async-done | bytes 3145744 | tf_op jit(solution)/shard_map/all_gather | solution.py:60
  1221.5 258.5 %while.55 = (s32[]{:T(128)}, f32[2,12,384,64]{2,3,1,0:T(8,128)}, bf16[2,12,1536,64]{2,3,1,0:T(8,128)(2,1)}, bf16[2,12,1536,64]{2,3,1,0:T(8,128)(2,1)}, bf16[2,12...) while((s32[]{:T(128)}, f32[2,12,384,64]{2,3,1,0:T(8,128)}, ...), condition=%wide.region_21.22_spmd, body=%wide.region_17.21_spmd.sunk | while | flops 382918272 | bytes 75056560 | solution.py:287
  1238.3 105.7 %while.57 = (s32[]{:T(128)}, f32[12,384,64]{1,2,0:T(8,128)}, bf16[12,1536,64]{1,2,0:T(8,128)(2,1)}, bf16[12,1536,64]{1,2,0:T(8,128)(2,1)}, bf16[12,384,64]{2,1,0...) while((s32[]{:T(128)}, f32[12,384,64]{1,2,0:T(8,128)}, ...), condition=%wide.region_20.20_spmd, body=%wide.region_18.19_spmd.sunk | while | flops 382918272 | bytes 20755576 | solution.py:285
  1367.5 105.7 %while.57 = (s32[]{:T(128)}, f32[12,384,64]{1,2,0:T(8,128)}, bf16[12,1536,64]{1,2,0:T(8,128)(2,1)}, bf16[12,1536,64]{1,2,0:T(8,128)(2,1)}, bf16[12,384,64]{2,1,0...) while((s32[]{:T(128)}, f32[12,384,64]{1,2,0:T(8,128)}, ...), condition=%wide.region_20.20_spmd, body=%wide.region_18.19_spmd.sunk | while | flops 382918272 | bytes 20755576 | solution.py:285
  1480.0 12.5 copy.128
  1498.0 9.3 copy.116
  1507.3 210.1 %copy.126 = bf16[2,1536,768]{0,2,1:T(8,128)(2,1)} copy(bf16[2,1536,768]{1,0,2:T(2,128)(2,1)} %bitcast.319) | data formatting | bytes 9437184
  1717.3 484.4 %reshape.444 = bf16[1536,1536]{1,0:T(8,128)(2,1)} reshape(bf16[1536,768,2]{2,1,0:T(8,128)(2,1)} %bitcast.94) | data formatting | bytes 9437184
  2223.3 63.9 %reduce-scatter.34.cloned.1.call-done = bf16[384,1536]{1,0:T(8,128)(2,1)} async-done(((bf16[1536,1536]{1,0:T(8,128)(2,1)}), bf16[384,1536]{1,0:T(8,128)(2,1)}) %reduce-scatter.34.cloned.1.call-update) | async-done | bytes 1179664
  2287.2 164.0 %reshape.445 = bf16[384,768,2]{2,1,0:T(8,128)(2,1)} reshape(bf16[384,1536]{1,0:T(8,128)(2,1)} %reduce-scatter.34.cloned.1.call-done) | data formatting | bytes 2359296
  2451.2 67.8 %copy.127 = bf16[2,384,768]{1,0,2:T(2,128)(2,1)S(1)} copy(bf16[2,384,768]{0,2,1:T(8,128)(2,1)} %bitcast.95) | data formatting | bytes 2359296
  2552.2 19.6 convolution_convert_fusion
  2571.9 20.8 copy.132
  2592.7 20.1 convolution_convert_fusion.1
  2612.9 19.8 convolution_convert_fusion.2
  2674.4 18.7 fusion.94
  2693.2 32.1 all-reduce.11.cloned.1.call-done
  2725.3 68.9 %reduce-scatter.38.cloned.1.call-done = bf16[128,768]{1,0:T(8,128)(2,1)} async-done(((bf16[2048,768]{1,0:T(8,128)(2,1)}), bf16[128,768]{1,0:T(8,128)(2,1)}) %reduce-scatter.38.cloned.1.call-update) | async-done | bytes 196624
  2796.0 179.6 %reduce-scatter.40.cloned.1.call-done = bf16[128,4096]{1,0:T(8,128)(2,1)} async-done(((bf16[2048,4096]{1,0:T(8,128)(2,1)}), bf16[128,4096]{1,0:T(8,128)(2,1)}) %reduce-scatter.40.cloned.1.call-update) | async-done | bytes 1048592
  2978.7 178.6 %reduce-scatter.32.cloned.1.call-done = bf16[128,4096]{1,0:T(8,128)(2,1)} async-done(((bf16[2048,4096]{1,0:T(8,128)(2,1)}), bf16[128,4096]{1,0:T(8,128)(2,1)}) %reduce-scatter.32.cloned.1.call-update) | async-done | bytes 1048592 | tf_op jit(solution)/shard_map/reduce_scatter | solution.py:366
  3160.1 178.8 %reduce-scatter.30.cloned.1.call-done = bf16[128,4096]{1,0:T(8,128)(2,1)} async-done(((bf16[2048,4096]{1,0:T(8,128)(2,1)}), bf16[128,4096]{1,0:T(8,128)(2,1)}) %reduce-scatter.30.cloned.1.call-update) | async-done | bytes 1048592 | tf_op jit(solution)/shard_map/reduce_scatter | solution.py:363
  3341.6 66.3 %reduce-scatter.28.cloned.1.call-done = bf16[128,768]{1,0:T(8,128)(2,1)} async-done(((bf16[2048,768]{1,0:T(8,128)(2,1)}), bf16[128,768]{1,0:T(8,128)(2,1)}) %reduce-scatter.28.cloned.1.call-update) | async-done | bytes 196624 | tf_op jit(solution)/shard_map/reduce_scatter | solution.py:357
  3409.6 76.6 %reduce-scatter.26.cloned.1.call-done = f32[384,2048]{1,0:T(8,128)} async-done(((f32[768,2048]{1,0:T(8,128)}), f32[384,2048]{1,0:T(8,128)}) %reduce-scatter.26.cloned.1.call-update) | async-done | bytes 3145744 | tf_op jit(solution)/shard_map/reduce_scatter | solution.py:65
  3489.1 37.0 %all-reduce.4 = (f32[2048]{0:T(1024)S(1)}, f32[2048]{0:T(1024)S(1)}, f32[64]{0:T(128)S(1)}, f32[64]{0:T(128)S(1)}) all-reduce(f32[2048]{0:T(1024)S(1)} %get-tuple-element.259, f32[2048]{0:T(1024)S(1)} %copy-done.50, f32[64]{0:T(128)S(1)} %get-tuple-element.257, f32[64]{0:T(128)S(1)} %copy-done.69), channel_id=1, replica_groups=mesh['dp'=4,'ctx'=4,'tp'=2] {'ctx','tp'}, use_global_device_ids=true, to_apply=%region_29.30 | all-reduce | flops 4224 | bytes 33792 | tf_op jit(solution)/shard_map/psum | solution.py:374
  3526.1 11.6 all-reduce.6
  3537.8 29.1 reduce-scatter.22.cloned.1.call-done
  3574.5 97.3 %all-reduce.13.cloned.1.call-done = (f32[2048,320]{0,1:T(8,128)}, f32[2048,320]{0,1:T(8,128)}) async-done(((f32[2048,320]{0,1:T(8,128)}, f32[2048,320]{0,1:T(8,128)}), (f32[2048,320]{0,1:T(8,128)}, f32[2048,320]{0,1:T(8,128)})) %all-reduce.13.cloned.1.call-update) | async-done | bytes 5242896 | tf_op jit(solution)/shard_map/psum | solution.py:373
  (668 shorter events, 627.2 us)
Async XLA Ops:
  7.2 7.6 copy-start
  7.2 53.3 %all-gather.12.cloned.1.call-start = ((), (), s32[]{:S(2)}) async-start(), calls=%async_computation.11 | async-start | bytes 4718592 | tf_op jit(solution)/shard_map/all_gather | solution.py:60
  12.7 95.3 %all-gather.14.cloned.1.call-start = ((), (), s32[]{:S(2)}) async-start(), calls=%async_computation.12 | async-start | bytes 3342336 | tf_op jit(solution)/shard_map/all_gather | solution.py:147
  13.4 185.0 %all-gather.18.cloned.1.call-start = ((), (), s32[]{:S(2)}) async-start(), calls=%async_computation.14 | async-start | bytes 5898240 | tf_op jit(solution)/shard_map/all_gather | solution.py:196
  14.8 53.6 %copy-start.59 = (s32[12]{0:T(128)}, s32[12]{0:T(128)S(1)}, u32[]{:S(2)}) copy-start(s32[12]{0:T(128)S(1)} %fusion.89) | copy-start | bytes 148
  67.4 220.9 %all-gather.16.cloned.1.call-start = ((), (), s32[]{:S(2)}) async-start(), calls=%async_computation.13 | async-start | bytes 5898240 | tf_op jit(solution)/shard_map/all_gather | solution.py:195
  72.6 47.2 %copy-start.29 = (f32[768,32]{0,1:T(8,128)}, f32[768,32]{0,1:T(8,128)S(1)}, u32[]{:S(2)}) copy-start(f32[768,32]{0,1:T(8,128)S(1)} %get-tuple-element.377) | copy-start | bytes 294916
  72.6 47.2 %copy-start.31 = (f32[768,32]{0,1:T(8,128)}, f32[768,32]{0,1:T(8,128)S(1)}, u32[]{:S(2)}) copy-start(f32[768,32]{0,1:T(8,128)S(1)} %get-tuple-element.378) | copy-start | bytes 294916
  76.8 35.9 copy-start.41
  76.8 41.7 %copy-start.35 = (f32[768,12]{0,1:T(8,128)}, f32[768,12]{0,1:T(8,128)S(1)}, u32[]{:S(2)}) copy-start(f32[768,12]{0,1:T(8,128)S(1)} %fusion.72) | copy-start | bytes 110596
  112.6 5.8 copy-start.61
  112.6 5.8 copy-start.63
  123.0 318.7 %all-gather.20.cloned.1.call-start = ((), (), s32[]{:S(2)}) async-start(), calls=%async_computation.15 | async-start | bytes 3342336 | tf_op jit(solution)/shard_map/all_gather | solution.py:148
  123.6 400.2 %reduce-scatter.20.cloned.1.call-start = ((), (), s32[]{:S(2)}) async-start(), calls=%async_computation.16 | async-start | bytes 9437184 | tf_op jit(solution)/shard_map/reduce_scatter | solution.py:65
  299.7 134.3 %copy-start.65 = (f32[12]{0:T(128)S(1)}, f32[12]{0:T(128)}, u32[]{:S(2)}) copy-start(f32[12]{0:T(128)} %compare_convert_fusion.2) | copy-start | bytes 148
  434.0 14.2 copy-start.8
  448.1 75.7 %copy-start.10 = (bf16[2,192,2048]{2,1,0:T(8,128)(2,1)S(1)}, bf16[2,192,2048]{2,1,0:T(8,128)(2,1)}, u32[]{:S(2)}) copy-start(bf16[2,192,2048]{2,1,0:T(8,128)(2,1)} %param.23) | copy-start | bytes 4718596
  448.2 126.3 %all-gather.22.cloned.1.call-start = ((), (), s32[]{:S(2)}) async-start(), calls=%async_computation.17 | async-start | bytes 4718592 | tf_op jit(solution)/shard_map/all_gather | solution.py:60
  529.4 174.5 %all-gather.26.cloned.1.call-start = ((), (), s32[]{:S(2)}) async-start(), calls=%async_computation.19 | async-start | bytes 17825792 | tf_op jit(solution)/shard_map/all_gather | solution.py:150
  530.1 301.2 %all-gather.24.cloned.1.call-start = ((), (), s32[]{:S(2)}) async-start(), calls=%async_computation.18 | async-start | bytes 17825792 | tf_op jit(solution)/shard_map/all_gather | solution.py:149
  530.9 345.1 %all-gather.30.cloned.1.call-start = ((), (), s32[]{:S(2)}) async-start(), calls=%async_computation.22 | async-start | bytes 4718592 | tf_op jit(solution)/shard_map/all_gather | solution.py:60
  531.4 477.1 %all-gather.28.cloned.1.call-start = ((), (), s32[]{:S(2)}) async-start(), calls=%async_computation.20 | async-start | bytes 17825792 | tf_op jit(solution)/shard_map/all_gather | solution.py:151
  532.2 628.2 %reduce-scatter.24.cloned.1.call-start = ((), (), s32[]{:S(2)}) async-start(), calls=%async_computation.23 | async-start | bytes 9437184 | tf_op jit(solution)/shard_map/reduce_scatter | solution.py:65
  1085.0 75.4 %copy-start.44 = (f32[2048]{0:T(1024)S(1)}, f32[2048]{0:T(1024)}, u32[]{:S(2)}) copy-start(f32[2048]{0:T(1024)} %param.28) | copy-start | bytes 24580
  1085.0 75.4 %copy-start.48 = (f32[2,192]{1,0:T(2,128)S(1)}, f32[2,192]{1,0:T(2,128)}, u32[]{:S(2)}) copy-start(f32[2,192]{1,0:T(2,128)} %copy-done.47) | copy-start | bytes 4612
  1085.0 79.8 %copy-start.17 = (bf16[2,192,2048]{2,1,0:T(8,128)(2,1)S(1)}, bf16[2,192,2048]{2,1,0:T(8,128)(2,1)}, u32[]{:S(2)}) copy-start(bf16[2,192,2048]{2,1,0:T(8,128)(2,1)} %param.24) | copy-start | bytes 4718596
  1085.0 127.4 %all-gather.32.cloned.1.call-start = ((), (), s32[]{:S(2)}) async-start(), calls=%async_computation.24 | async-start | bytes 4718592 | tf_op jit(solution)/shard_map/all_gather | solution.py:60
  1167.3 1037.8 %reduce-scatter.36.cloned.1.call-start = ((), (), s32[]{:S(2)}) async-start(), calls=%async_computation.30 | async-start | bytes 5898240
  1229.0 6.8 copy-start.2
  1358.2 6.8 copy-start.2
  1497.9 789.3 %reduce-scatter.34.cloned.1.call-start = ((), (), s32[]{:S(2)}) async-start(), calls=%async_computation.29 | async-start | bytes 5898240
  2201.8 523.5 %all-reduce.11.cloned.1.call-start = ((), (), s32[]{:S(2)}) async-start(), calls=%async_computation.33 | async-start | bytes 10485760 | tf_op jit(solution)/shard_map/psum | solution.py:374
  2540.3 253.9 %reduce-scatter.38.cloned.1.call-start = ((), (), s32[]{:S(2)}) async-start(), calls=%async_computation.31 | async-start | bytes 3342336
  2552.2 423.5 %reduce-scatter.40.cloned.1.call-start = ((), (), s32[]{:S(2)}) async-start(), calls=%async_computation.32 | async-start | bytes 17825792
  2592.6 564.7 %reduce-scatter.32.cloned.1.call-start = ((), (), s32[]{:S(2)}) async-start(), calls=%async_computation.28 | async-start | bytes 17825792 | tf_op jit(solution)/shard_map/reduce_scatter | solution.py:366
  2612.8 726.0 %reduce-scatter.30.cloned.1.call-start = ((), (), s32[]{:S(2)}) async-start(), calls=%async_computation.27 | async-start | bytes 17825792 | tf_op jit(solution)/shard_map/reduce_scatter | solution.py:363
  2632.6 775.3 %reduce-scatter.28.cloned.1.call-start = ((), (), s32[]{:S(2)}) async-start(), calls=%async_computation.26 | async-start | bytes 3342336 | tf_op jit(solution)/shard_map/reduce_scatter | solution.py:357
  2642.4 7.9 copy-start.20
  2642.4 843.8 %reduce-scatter.26.cloned.1.call-start = ((), (), s32[]{:S(2)}) async-start(), calls=%async_computation.25 | async-start | bytes 9437184 | tf_op jit(solution)/shard_map/reduce_scatter | solution.py:65
  2671.1 895.7 %reduce-scatter.22.cloned.1.call-start = ((), (), s32[]{:S(2)}) async-start(), calls=%async_computation.21 | async-start | bytes 9437184 | tf_op jit(solution)/shard_map/reduce_scatter | solution.py:65
  2693.1 978.7 %all-reduce.13.cloned.1.call-start = ((), (), s32[]{:S(2)}) async-start(), calls=%async_computation.34 | async-start | bytes 10485760 | tf_op jit(solution)/shard_map/psum | solution.py:373
  3160.1 326.1 %copy-start.11 = (bf16[2,192,2048]{2,1,0:T(8,128)(2,1)S(1)}, bf16[2,192,2048]{2,1,0:T(8,128)(2,1)}, u32[]{:S(2)}) copy-start(bf16[2,192,2048]{2,1,0:T(8,128)(2,1)} %param.23) | copy-start | bytes 4718596
  3160.1 326.1 %copy-start.46 = (f32[2048]{0:T(1024)S(1)}, f32[2048]{0:T(1024)}, u32[]{:S(2)}) copy-start(f32[2048]{0:T(1024)} %param.27) | copy-start | bytes 24580
  3160.1 326.1 %copy-start.52 = (f32[2,192]{1,0:T(2,128)S(1)}, f32[2,192]{1,0:T(2,128)}, u32[]{:S(2)}) copy-start(f32[2,192]{1,0:T(2,128)} %copy-done.51) | copy-start | bytes 4612
  3486.2 51.5 %copy-start.54 = (f32[2,192]{1,0:T(2,128)S(1)}, f32[2,192]{1,0:T(2,128)}, u32[]{:S(2)}) copy-start(f32[2,192]{1,0:T(2,128)} %copy-done.53) | copy-start | bytes 4612
  3486.2 80.6 %copy-start.45 = (f32[2048]{0:T(1024)S(1)}, f32[2048]{0:T(1024)}, u32[]{:S(2)}) copy-start(f32[2048]{0:T(1024)} %param.28) | copy-start | bytes 24580
  3486.2 80.6 %copy-start.49 = (f32[2,192]{1,0:T(2,128)S(1)}, f32[2,192]{1,0:T(2,128)}, u32[]{:S(2)}) copy-start(f32[2,192]{1,0:T(2,128)} %copy-done.47) | copy-start | bytes 4612
  3486.3 80.6 %copy-start.58 = (f32[2,192]{1,0:T(2,128)S(1)}, f32[2,192]{1,0:T(2,128)}, u32[]{:S(2)}) copy-start(f32[2,192]{1,0:T(2,128)} %copy-done.57) | copy-start | bytes 4612
  (57 other events, 158.9 us)
Sparse Core Ops, SparseCore 0:
  12.8 47.6 all-gather.11
  62.8 45.1 all-gather.13
  110.2 88.1 all-gather.17
  200.4 87.8 all-gather.15
  290.2 46.6 all-gather.19
  448.3 75.4 reduce-scatter.19
  529.5 44.9 all-gather.21
  576.9 126.8 all-gather.25
  706.3 124.9 all-gather.23
  832.8 43.0 all-gather.29
  878.2 130.3 all-gather.27
  1085.1 75.2 reduce-scatter.23
  1167.4 44.9 all-gather.31
  1498.0 85.2 reduce-scatter.35
  2201.9 85.2 reduce-scatter.33
  2540.4 184.8 all-reduce.10
  2728.9 65.1 reduce-scatter.37
  2798.1 177.4 reduce-scatter.39
  2979.7 177.5 reduce-scatter.31
  3161.3 177.5 reduce-scatter.29
  3342.6 65.2 reduce-scatter.27
  3410.2 75.9 reduce-scatter.25
  3488.6 78.1 reduce-scatter.21
  3569.1 102.6 all-reduce.12
